TPU v7x, 256 devices: a whole 4x4x8 slice. The times are simulated.
256 devices in a mesh: rows: 64 (over x, z, core), cols: 4 (over y).
Axes of the slice: x: 4, y: 4, z: 8, core: 2. Of those that a mesh axis runs over, the one named last changes fastest.
Arguments:
- kernel: float32 [16384, 16384], P('rows', 'cols'), may hold values from 0 to 2, as said below
- row_block: int32 [256], P('rows'), may hold values from 0 to 255, as said below
- panel_order: int32 [2], replicated, may hold values from 0 to 63, as said below
- samples: float32 [16384, 512], P('rows', 'cols'), may hold values from -6 to 6
Outputs:
- trailing: float32 [16384, 16384], P('rows', 'cols')
- factor: float32 [16384, 512], P('rows')
- solved: float32 [512, 512], P(None, 'cols')
- reduced_samples: float32 [16384, 512], P('rows', 'cols')
Inputs may be any that keep to these rules, and one draw needn't show every extreme that they name: `row_block`: the stored row blocks of rows index i (stored blocks i * 4 to (i + 1) * 4 - 1) hold the global row blocks i + t * 64, t = 0 .. 3, each once, in some order. `panel_order`: the entries are distinct, and one of them is 63. `kernel`: in global row order the matrix is symmetric and positive definite, its smallest eigenvalue 0.25 or more.
All inputs are finite; a program needn't handle non-finite values.
Results may differ from a plain program's by a relative error of at most 0.0003.
Values sent between devices are 32-bit elements; how exact they have to be, the bound alone decides.
No kernel may reach another device: no remote copies, remote signals or barrier semaphores. Data moves between devices by JAX's collectives and lax.ppermute only.
A program may use at most 128 MiB of HBM per device.

v0:
```python
import jax
import jax.numpy as jnp
from jax import lax
from jax.sharding import PartitionSpec as P

PW = 256
PANELS = 2
EXACT = lax.Precision.HIGHEST


def broadcast(block, axis, owner):
    block = jnp.where(lax.axis_index(axis) == owner, block, jnp.zeros_like(block))
    return lax.psum(block, axis)


def times_transposed(left_side, right_side):
    return lax.dot_general(
        left_side,
        right_side,
        (((1,), (1,)), ((), ())),
        precision=EXACT,
        preferred_element_type=jnp.float32,
    )


def matmul_plain(left_side, right_side):
    return jnp.dot(left_side, right_side, precision=EXACT, preferred_element_type=jnp.float32)


def stored_order(array, restore, blocks_here):
    width_here = array.shape[1]
    return jnp.take(array.reshape(blocks_here, -1, width_here), restore, axis=0).reshape(
        array.shape
    )


def on_device(kernel, row_block, panel_order, samples):
    rows_count = lax.axis_size("rows")
    cols_count = lax.axis_size("cols")
    cols_place = lax.axis_index("cols")
    blocks_here = row_block.shape[0]
    local_rows, local_cols = kernel.shape
    block_rows = local_rows // blocks_here
    per_panel = PW // block_rows
    share = blocks_here // cols_count
    right_cols = samples.shape[1]
    ranking = jnp.argsort(row_block)
    restore = jnp.argsort(ranking)
    sorted_blocks = jnp.take(row_block, ranking)
    trailing_work = jnp.take(
        kernel.reshape(blocks_here, block_rows, local_cols), ranking, axis=0
    ).reshape(local_rows, local_cols)
    right_side = jnp.take(
        samples.reshape(blocks_here, block_rows, right_cols), ranking, axis=0
    ).reshape(local_rows, right_cols)
    identity = jnp.eye(PW, dtype=jnp.float32)
    factors = []
    solutions = []
    for panel_step in range(PANELS):
        panel_start = panel_order[panel_step] * PW
        column_owner = panel_start // local_cols
        offset = panel_start - column_owner * local_cols
        own_columns = lax.dynamic_slice_in_dim(trailing_work, offset, PW, 1)
        columns = broadcast(own_columns, "cols", column_owner)
        first_block = panel_order[panel_step] * per_panel
        wanted = first_block + jnp.arange(per_panel, dtype=jnp.int32)
        chooser = (wanted[:, None] == sorted_blocks[None, :]).astype(jnp.float32)
        diag_part = jnp.einsum(
            "ot,trp->orp", chooser, columns.reshape(blocks_here, block_rows, PW), precision=EXACT
        ).reshape(PW, PW)
        right_part = jnp.einsum(
            "ot,trp->orp",
            chooser,
            right_side.reshape(blocks_here, block_rows, right_cols),
            precision=EXACT,
        ).reshape(PW, right_cols)
        diagonal, panel_right = lax.psum((diag_part, right_part), "rows")
        lower_factor = jnp.linalg.cholesky(diagonal)
        inverse = jax.scipy.linalg.solve_triangular(lower_factor, identity, lower=True)
        factor_own = times_transposed(columns, inverse)
        solved_now = matmul_plain(inverse, panel_right)
        right_side = right_side - matmul_plain(factor_own, solved_now)
        my_piece = lax.dynamic_slice_in_dim(
            factor_own, cols_place * share * block_rows, share * block_rows, 0
        )
        spread = times_transposed(factor_own, lax.all_gather(my_piece, "rows", axis=0, tiled=True))
        update = (
            spread.reshape(local_rows, rows_count, share, block_rows)
            .transpose(0, 2, 1, 3)
            .reshape(local_rows, local_cols)
        )
        trailing_work = trailing_work - update
        factors.append(factor_own)
        solutions.append(solved_now)
    factor_all = jnp.concatenate(factors, 1)
    return (
        stored_order(trailing_work, restore, blocks_here),
        stored_order(factor_all, restore, blocks_here),
        jnp.concatenate(solutions, 0),
        stored_order(right_side, restore, blocks_here),
    )


def solution(mesh):
    in_specs = (P("rows", "cols"), P("rows"), P(), P("rows", "cols"))
    out_specs = (P("rows", "cols"), P("rows", None), P(None, "cols"), P("rows", "cols"))
    return jax.shard_map(
        on_device, mesh=mesh, in_specs=in_specs, out_specs=out_specs, check_vma=False
    )
```

profile of v0, /device:TPU:1, one launch (start us, length us, event | category | flops | bytes accessed | tf_op | source)
XLA Modules:
  0.0 816.9 jit_solution(4630192233342211881)
XLA Ops:
  7.2 1.3 fusion.51
  9.2 1.4 sort.31
  10.6 1.3 gather_fusion
  11.9 5.0 gather_fusion.2
  16.9 2.7 broadcast_select_fusion.1
  19.6 2.0 copy-done.2
  21.6 0.7 dynamic-slice_select_fusion.1
  23.0 0.6 gather_fusion.4
  24.0 0.7 copy.24
  24.7 46.3 %all-reduce.8.cloned.1.call-done = f32[256,256]{1,0:T(8,128)} async-done(((f32[256,256]{1,0:T(8,128)}), f32[256,256]{1,0:T(8,128)}) %all-reduce.8.cloned.1.call-update) | async-done | bytes 262160 | tf_op jit(solution)/shard_map/psum | solution.py:13
  71.0 1.5 fusion.4
  72.6 0.8 copy.17
  73.6 183.5 %all-reduce.14.cloned.1.call-done = (f32[256,256]{0,1:T(8,128)}, f32[256,128]{1,0:T(8,128)}) async-done(((f32[256,256]{0,1:T(8,128)}, f32[256,128]{1,0:T(8,128)}), (f32[256,256]{0,1:T(8,128)}, f32[256,128]{1,0:T(8,128)})) %all-reduce.14.cloned.1.call-update) | async-done | bytes 393232 | tf_op jit(solution)/shard_map/psum | solution.py:77
  257.1 1.1 copy.18
  258.2 1.0 fusion.1
  259.2 11.7 %cholesky.130 = f32[128,128]{1,0:T(8,128)S(1)} custom-call(f32[128,128]{1,0:T(8,128)S(1)} %cholesky.194), custom_call_target="Cholesky" | custom-call | tf_op jit(solution)/shard_map/jit(cholesky)/cholesky | solution.py:78
  271.0 9.8 %custom-call.13 = f32[1,128,128]{1,2,0:T(8,128)S(1)} custom-call(f32[1,128,128]{2,1,0:T(8,128)S(1)} %get-tuple-element.61), custom_call_target="InvertDiagBlocksLowerTriangular" | custom-call | tf_op jit(solution)/shard_map/jit(cholesky)/cholesky | solution.py:78
  281.3 11.7 %cholesky.147 = f32[128,128]{1,0:T(8,128)S(1)} custom-call(f32[128,128]{1,0:T(8,128)S(1)} %convolution_subtract_fusion.7), custom_call_target="Cholesky" | custom-call | tf_op jit(solution)/shard_map/jit(cholesky)/cholesky | solution.py:78
  293.1 0.6 compare_reduce_fusion.2
  295.1 4.5 while.4
  295.6 0.6 fusion.74
  296.2 1.4 bitcast_dynamic-update-slice_fusion.4
  297.6 0.6 fusion.74
  298.2 1.4 bitcast_dynamic-update-slice_fusion.4
  299.6 19.7 %custom-call.14 = f32[2,128,128]{1,2,0:T(8,128)S(1)} custom-call(f32[2,128,128]{2,1,0:T(8,128)S(1)} %get-tuple-element.26), custom_call_target="InvertDiagBlocksLowerTriangular" | custom-call | tf_op jit(solution)/shard_map/jit(_solve_triangular)/triangular_solve | solution.py:79
  320.2 0.4 fusion.10
  320.6 0.6 constant_dynamic-slice_fusion.3
  322.7 0.4 fusion.9
  323.1 78.1 %all-gather.3.cloned.1.call-done = f32[4096,256]{1,0:T(8,128)} async-done(((f32[64,256]{1,0:T(8,128)}), f32[4096,256]{1,0:T(8,128)}) %all-gather.3.cloned.1.call-update) | async-done | bytes 4194320 | tf_op jit(solution)/shard_map/all_gather | solution.py:86
  401.1 11.4 %convolution_subtract_fusion.1 = f32[256,4096]{1,0:T(8,128)S(1)} fusion(f32[256,4096]{1,0:T(8,128)} %bitcast.108, f32[256,256]{1,0:T(8,128)S(1)} %fusion.10, f32[4096,256]{1,0:T(8,128)} %all-gather.3.cloned.1.call-done), kind=kOutput, calls=%fused_computation.11 | convolution fusion | flops 3222274048 | bytes 12845056 | tf_op jit(solution)/shard_map/dot_general | solution.py:17
  412.6 2.0 copy-done.1
  414.6 0.7 dynamic-slice_select_fusion
  415.4 0.4 convolution_subtract_fusion.3
  416.1 0.7 copy.26
  416.8 40.3 %all-reduce.10.cloned.1.call-done = f32[256,256]{1,0:T(8,128)} async-done(((f32[256,256]{1,0:T(8,128)}), f32[256,256]{1,0:T(8,128)}) %all-reduce.10.cloned.1.call-update) | async-done | bytes 262160 | tf_op jit(solution)/shard_map/psum | solution.py:13
  457.1 1.5 fusion.2
  458.7 0.8 copy.21
  459.8 183.3 %all-reduce.12.cloned.1.call-done = (f32[256,256]{0,1:T(8,128)}, f32[256,128]{1,0:T(8,128)}) async-done(((f32[256,256]{0,1:T(8,128)}, f32[256,128]{1,0:T(8,128)}), (f32[256,256]{0,1:T(8,128)}, f32[256,128]{1,0:T(8,128)})) %all-reduce.12.cloned.1.call-update) | async-done | bytes 393232 | tf_op jit(solution)/shard_map/psum | solution.py:77
  643.0 1.1 copy.22
  644.2 1.0 fusion
  645.2 11.7 %cholesky.164 = f32[128,128]{1,0:T(8,128)S(1)} custom-call(f32[128,128]{1,0:T(8,128)S(1)} %cholesky.197), custom_call_target="Cholesky" | custom-call | tf_op jit(solution)/shard_map/jit(cholesky)/cholesky | solution.py:78
  656.9 9.8 %custom-call.15 = f32[1,128,128]{1,2,0:T(8,128)S(1)} custom-call(f32[1,128,128]{2,1,0:T(8,128)S(1)} %get-tuple-element.57), custom_call_target="InvertDiagBlocksLowerTriangular" | custom-call | tf_op jit(solution)/shard_map/jit(cholesky)/cholesky | solution.py:78
  667.2 11.7 %cholesky.181 = f32[128,128]{1,0:T(8,128)S(1)} custom-call(f32[128,128]{1,0:T(8,128)S(1)} %convolution_subtract_fusion.6), custom_call_target="Cholesky" | custom-call | tf_op jit(solution)/shard_map/jit(cholesky)/cholesky | solution.py:78
  679.0 0.6 compare_reduce_fusion
  679.6 0.6 compare_reduce_fusion.1
  681.6 4.2 while.5
  681.8 0.6 fusion.75
  682.4 1.4 bitcast_dynamic-update-slice_fusion.5
  683.8 0.6 fusion.75
  684.4 1.4 bitcast_dynamic-update-slice_fusion.5
  685.8 19.7 %custom-call.16 = f32[2,128,128]{1,2,0:T(8,128)S(1)} custom-call(f32[2,128,128]{2,1,0:T(8,128)S(1)} %get-tuple-element.27), custom_call_target="InvertDiagBlocksLowerTriangular" | custom-call | tf_op jit(solution)/shard_map/jit(_solve_triangular)/triangular_solve | solution.py:79
  706.4 0.4 fusion.8
  706.8 0.6 constant_dynamic-slice_fusion.2
  707.5 0.7 sort.32
  708.4 0.4 fusion.7
  709.2 0.6 gather_fusion.5
  709.8 0.6 gather_fusion.1
  710.4 0.7 pad_maximum_fusion.3
  711.2 0.7 broadcast_select_fusion.2
  711.9 0.9 bitcast_select_fusion
  712.8 74.6 %all-gather.5.cloned.1.call-done = f32[4096,256]{1,0:T(8,128)} async-done(((f32[64,256]{1,0:T(8,128)}), f32[4096,256]{1,0:T(8,128)}) %all-gather.5.cloned.1.call-update) | async-done | bytes 4194320 | tf_op jit(solution)/shard_map/all_gather | solution.py:86
  787.4 12.7 %convolution_subtract_fusion = f32[256,4096]{1,0:T(8,128)} fusion(f32[256,4096]{1,0:T(8,128)} %copy-done.1, f32[256,256]{1,0:T(8,128)S(1)} %fusion.8, f32[4096,256]{1,0:T(8,128)} %all-gather.5.cloned.1.call-done), kind=kOutput, calls=%fused_computation.10 | convolution fusion | flops 3222274048 | bytes 12845056 | tf_op jit(solution)/shard_map/dot_general | solution.py:17
  800.1 4.9 gather_fusion.3
  805.0 4.8 broadcast_select_fusion
  (72 shorter events, 5.1 us)
Async XLA Ops:
  7.2 15.9 %copy-start = (f32[256,128]{1,0:T(8,128)S(1)}, f32[256,128]{1,0:T(8,128)}, u32[]{:S(2)}) copy-start(f32[256,128]{1,0:T(8,128)} %param.14) | copy-start | bytes 393220
  7.2 63.8 %all-reduce.8.cloned.1.call-start = ((), (), s32[]{:S(2)}) async-start(), calls=%async_computation | async-start | bytes 524288 | tf_op jit(solution)/shard_map/psum | solution.py:13
  19.6 2.0 copy-start.2
  22.4 234.8 %all-reduce.14.cloned.1.call-start = ((), (), s32[]{:S(2)}) async-start(), calls=%async_computation.5 | async-start | bytes 786432 | tf_op jit(solution)/shard_map/psum | solution.py:77
  71.0 249.2 %copy-start.3 = (f32[256,256]{1,0:T(8,128)S(1)}, f32[256,256]{1,0:T(8,128)}, u32[]{:S(2)}) copy-start(f32[256,256]{1,0:T(8,128)} %all-reduce.8.cloned.1.call-done) | copy-start | bytes 786436
  73.5 327.7 %all-gather.3.cloned.1.call-start = ((), (), s32[]{:S(2)}) async-start(), calls=%async_computation.1 | async-start | bytes 4259840 | tf_op jit(solution)/shard_map/all_gather | solution.py:86
  257.1 65.6 %copy-start.5 = (f32[256,128]{1,0:T(8,128)S(1)}, f32[256,128]{1,0:T(8,128)}, u32[]{:S(2)}) copy-start(f32[256,128]{1,0:T(8,128)} %get-tuple-element.47) | copy-start | bytes 393220
  321.3 135.8 %all-reduce.10.cloned.1.call-start = ((), (), s32[]{:S(2)}) async-start(), calls=%async_computation.2 | async-start | bytes 524288 | tf_op jit(solution)/shard_map/psum | solution.py:13
  412.6 2.0 copy-start.1
  415.3 227.7 %all-reduce.12.cloned.1.call-start = ((), (), s32[]{:S(2)}) async-start(), calls=%async_computation.4 | async-start | bytes 786432 | tf_op jit(solution)/shard_map/psum | solution.py:77
  457.1 249.3 %copy-start.4 = (f32[256,256]{1,0:T(8,128)S(1)}, f32[256,256]{1,0:T(8,128)}, u32[]{:S(2)}) copy-start(f32[256,256]{1,0:T(8,128)} %all-reduce.10.cloned.1.call-done) | copy-start | bytes 786436
  459.5 327.8 %all-gather.5.cloned.1.call-start = ((), (), s32[]{:S(2)}) async-start(), calls=%async_computation.3 | async-start | bytes 4259840 | tf_op jit(solution)/shard_map/all_gather | solution.py:86
  643.0 65.4 %copy-start.6 = (f32[256,128]{1,0:T(8,128)S(1)}, f32[256,128]{1,0:T(8,128)}, u32[]{:S(2)}) copy-start(f32[256,128]{1,0:T(8,128)} %get-tuple-element.45) | copy-start | bytes 393220
Sparse Core Ops, SparseCore 0:
  22.5 48.4 all-reduce.7
  75.5 181.5 all-reduce.13
  321.4 79.7 all-gather.2
  415.5 41.5 all-reduce.9
  461.4 181.5 all-reduce.11
  707.6 79.7 all-gather.4
where the time goes:
time: 826 us; the launch traced here: 817 us
  waiting for transfers between devices  606 us (73%)
  other arithmetic  124 us (15%)
  local copies, waits for them, and re-layouts  33.1 us (4%)
  matrix products  32.9 us (4%)
  between operations  20 us (2%)
    psum x2, waiting for transfers between devices, on_device(): diagonal, panel_right = lax.psum((diag_part, right_part), 'rows')  367 us
    all_gather x2, waiting for transfers between devices, on_device(): lax.all_gather(my_piece, 'rows', axis=0, tiled=True)  153 us
    psum x2, waiting for transfers between devices, broadcast(): return lax.psum(block, axis)  86.6 us
    another operation x13, other arithmetic, on_device(): lower_factor = jnp.linalg.cholesky(diagonal)  68.5 us
    another operation x5, other arithmetic, on_device(): jax.scipy.linalg.solve_triangular(lower_factor, identity, lower=True)  39.4 us
    dot_general x4, matrix products, times_transposed(): lax.dot_general(left_side, right_side, (((1,), (1,)), ((), ())), precisio...  25 us
  transfers between devices with their start and end apart: 6, of which 6 were waited for; matrix products, arithmetic and copies ran while one was open for 1% of the time, Pallas kernels for 0%

commit v1 on v0

--- a/solution.py
+++ b/solution.py
@@ -1,3 +1,4 @@
+import functools
 import jax
 import jax.numpy as jnp
 from jax import lax
@@ -6,6 +7,17 @@
 PW = 256
 PANELS = 2
 EXACT = lax.Precision.HIGHEST
+
+
+def ratios_get(unit, net_axis, row_dim):
+    n_shards = jax.lax.psum(1, net_axis)
+    bank = [n_shards if d == row_dim else 1 for d in range(unit.ndim)]
+    return jax.lax.all_to_all(
+        jnp.tile(unit, bank), net_axis, split_axis=row_dim, concat_axis=row_dim, tiled=True
+    )
+
+
+_begin_roads = functools.partial(ratios_get, net_axis="rows", row_dim=0)
 
 
 def broadcast(block, axis, owner):
@@ -83,7 +95,7 @@
         my_piece = lax.dynamic_slice_in_dim(
             factor_own, cols_place * share * block_rows, share * block_rows, 0
         )
-        spread = times_transposed(factor_own, lax.all_gather(my_piece, "rows", axis=0, tiled=True))
+        spread = times_transposed(factor_own, _begin_roads(my_piece))
         update = (
             spread.reshape(local_rows, rows_count, share, block_rows)
             .transpose(0, 2, 1, 3)

time: 826 us -> 881 us (1.067)
  waiting for transfers between devices: 606 us -> 638 us
  starting transfers between devices: 0.42 us -> 20.3 us
    all_to_all x0 -> x2, waiting for transfers between devices: none -> 185 us  [ratios_get(): jax.lax.all_to_all(jnp.tile(unit, bank), net_axis, split_axis=row_dim, co...]
    all_gather x2 -> x0, waiting for transfers between devices: 153 us -> none  [on_device(): lax.all_gather(my_piece, 'rows', axis=0, tiled=True)]
    all_to_all x0 -> x2, starting transfers between devices: none -> 19.9 us  [ratios_get(): jax.lax.all_to_all(jnp.tile(unit, bank), net_axis, split_axis=row_dim, co...]
where the time goes in v1:
time: 881 us; the launch traced here: 872 us
  waiting for transfers between devices  638 us (72%)
  other arithmetic  124 us (14%)
  local copies, waits for them, and re-layouts  36.7 us (4%)
  matrix products  32.9 us (4%)
  starting transfers between devices  20.3 us (2%)
  between operations  19.7 us (2%)
    psum x2, waiting for transfers between devices, on_device(): diagonal, panel_right = lax.psum((diag_part, right_part), 'rows')  367 us
    all_to_all x2, waiting for transfers between devices, ratios_get(): jax.lax.all_to_all(jnp.tile(unit, bank), net_axis, split_axis=row_dim, co...  185 us
    psum x2, waiting for transfers between devices, broadcast(): return lax.psum(block, axis)  85.9 us
    another operation x13, other arithmetic, on_device(): lower_factor = jnp.linalg.cholesky(diagonal)  68.5 us
    another operation x5, other arithmetic, on_device(): jax.scipy.linalg.solve_triangular(lower_factor, identity, lower=True)  39.4 us
    dot_general x4, matrix products, times_transposed(): lax.dot_general(left_side, right_side, (((1,), (1,)), ((), ())), precisio...  25 us
    all_to_all x2, starting transfers between devices, ratios_get(): jax.lax.all_to_all(jnp.tile(unit, bank), net_axis, split_axis=row_dim, co...  19.9 us
  transfers between devices with their start and end apart: 6, of which 6 were waited for; matrix products, arithmetic and copies ran while one was open for 1% of the time, Pallas kernels for 0%

profile of v1, /device:TPU:1, one launch (start us, length us, event | category | flops | bytes accessed | tf_op | source)
XLA Modules:
  0.0 871.7 jit_solution(16290925665993457061)
XLA Ops:
  7.2 1.3 fusion.51
  9.2 1.4 sort.31
  10.6 1.3 gather_fusion
  11.9 5.0 gather_fusion.2
  16.9 2.7 broadcast_select_fusion.1
  19.6 2.0 copy-done.2
  21.6 0.7 dynamic-slice_select_fusion.1
  23.0 0.6 gather_fusion.4
  24.0 0.7 copy.24
  24.7 46.3 %all-reduce.8.cloned.1.call-done = f32[256,256]{1,0:T(8,128)} async-done(((f32[256,256]{1,0:T(8,128)}), f32[256,256]{1,0:T(8,128)}) %all-reduce.8.cloned.1.call-update) | async-done | bytes 262160 | tf_op jit(solution)/shard_map/psum | solution.py:25
  71.0 1.5 fusion.4
  72.6 0.8 copy.17
  73.5 183.6 %all-reduce.14.cloned.1.call-done = (f32[256,256]{0,1:T(8,128)}, f32[256,128]{1,0:T(8,128)}) async-done(((f32[256,256]{0,1:T(8,128)}, f32[256,128]{1,0:T(8,128)}), (f32[256,256]{0,1:T(8,128)}, f32[256,128]{1,0:T(8,128)})) %all-reduce.14.cloned.1.call-update) | async-done | bytes 393232 | tf_op jit(solution)/shard_map/psum | solution.py:89
  257.1 1.1 copy.18
  258.2 1.0 fusion.1
  259.2 11.7 %cholesky.130 = f32[128,128]{1,0:T(8,128)S(1)} custom-call(f32[128,128]{1,0:T(8,128)S(1)} %cholesky.194), custom_call_target="Cholesky" | custom-call | tf_op jit(solution)/shard_map/jit(cholesky)/cholesky | solution.py:90
  271.0 9.8 %custom-call.13 = f32[1,128,128]{1,2,0:T(8,128)S(1)} custom-call(f32[1,128,128]{2,1,0:T(8,128)S(1)} %get-tuple-element.61), custom_call_target="InvertDiagBlocksLowerTriangular" | custom-call | tf_op jit(solution)/shard_map/jit(cholesky)/cholesky | solution.py:90
  281.3 11.7 %cholesky.147 = f32[128,128]{1,0:T(8,128)S(1)} custom-call(f32[128,128]{1,0:T(8,128)S(1)} %convolution_subtract_fusion.7), custom_call_target="Cholesky" | custom-call | tf_op jit(solution)/shard_map/jit(cholesky)/cholesky | solution.py:90
  293.0 0.6 compare_reduce_fusion.2
  295.1 4.5 while.4
  295.6 0.6 fusion.74
  296.2 1.4 bitcast_dynamic-update-slice_fusion.4
  297.6 0.6 fusion.74
  298.2 1.4 bitcast_dynamic-update-slice_fusion.4
  299.6 19.7 %custom-call.14 = f32[2,128,128]{1,2,0:T(8,128)S(1)} custom-call(f32[2,128,128]{2,1,0:T(8,128)S(1)} %get-tuple-element.26), custom_call_target="InvertDiagBlocksLowerTriangular" | custom-call | tf_op jit(solution)/shard_map/jit(_solve_triangular)/triangular_solve | solution.py:91
  320.2 0.4 fusion.10
  320.6 2.5 tile.4
  323.1 10.0 %all-to-all-start = ((f32[64,64,256]{2,1,0:T(8,128)}), f32[64,64,256]{2,1,0:T(8,128)}, u32[]{:S(2)}, u32[]{:S(2)}) async-start(f32[64,64,256]{2,1,0:T(8,128)} %tile.4), calls=%async_computation | async-start | bytes 8388608 | tf_op jit(solution)/shard_map/all_to_all | solution.py:15
  334.8 94.1 %all-to-all-done = f32[64,64,256]{2,1,0:T(8,128)} async-done(((f32[64,64,256]{2,1,0:T(8,128)}), f32[64,64,256]{2,1,0:T(8,128)}, u32[]{:S(2)}, u32[]{:S(2)}) %all-to-all-start) | async-done | bytes 4194336 | tf_op jit(solution)/shard_map/all_to_all | solution.py:15
  428.9 11.4 %convolution_subtract_fusion.1 = f32[256,4096]{1,0:T(8,128)S(1)} fusion(f32[256,4096]{1,0:T(8,128)} %bitcast.110, f32[256,256]{1,0:T(8,128)S(1)} %fusion.10, f32[4096,256]{1,0:T(8,128)} %bitcast.12), kind=kOutput, calls=%fused_computation.11 | convolution fusion | flops 3222274048 | bytes 12845056 | tf_op jit(solution)/shard_map/dot_general | solution.py:29
  440.4 2.0 copy-done.1
  442.4 0.7 dynamic-slice_select_fusion
  444.1 0.7 copy.26
  444.7 39.6 %all-reduce.10.cloned.1.call-done = f32[256,256]{1,0:T(8,128)} async-done(((f32[256,256]{1,0:T(8,128)}), f32[256,256]{1,0:T(8,128)}) %all-reduce.10.cloned.1.call-update) | async-done | bytes 262160 | tf_op jit(solution)/shard_map/psum | solution.py:25
  484.4 1.5 fusion.2
  486.0 0.8 copy.21
  486.9 183.5 %all-reduce.12.cloned.1.call-done = (f32[256,256]{0,1:T(8,128)}, f32[256,128]{1,0:T(8,128)}) async-done(((f32[256,256]{0,1:T(8,128)}, f32[256,128]{1,0:T(8,128)}), (f32[256,256]{0,1:T(8,128)}, f32[256,128]{1,0:T(8,128)})) %all-reduce.12.cloned.1.call-update) | async-done | bytes 393232 | tf_op jit(solution)/shard_map/psum | solution.py:89
  670.3 1.1 copy.22
  671.4 1.0 fusion
  672.4 11.7 %cholesky.164 = f32[128,128]{1,0:T(8,128)S(1)} custom-call(f32[128,128]{1,0:T(8,128)S(1)} %cholesky.197), custom_call_target="Cholesky" | custom-call | tf_op jit(solution)/shard_map/jit(cholesky)/cholesky | solution.py:90
  684.2 9.8 %custom-call.15 = f32[1,128,128]{1,2,0:T(8,128)S(1)} custom-call(f32[1,128,128]{2,1,0:T(8,128)S(1)} %get-tuple-element.57), custom_call_target="InvertDiagBlocksLowerTriangular" | custom-call | tf_op jit(solution)/shard_map/jit(cholesky)/cholesky | solution.py:90
  694.5 11.7 %cholesky.181 = f32[128,128]{1,0:T(8,128)S(1)} custom-call(f32[128,128]{1,0:T(8,128)S(1)} %convolution_subtract_fusion.6), custom_call_target="Cholesky" | custom-call | tf_op jit(solution)/shard_map/jit(cholesky)/cholesky | solution.py:90
  706.3 0.6 compare_reduce_fusion
  706.9 0.6 compare_reduce_fusion.1
  708.9 4.2 while.5
  709.1 0.6 fusion.75
  709.7 1.4 bitcast_dynamic-update-slice_fusion.5
  711.1 0.6 fusion.75
  711.7 1.4 bitcast_dynamic-update-slice_fusion.5
  713.1 19.7 %custom-call.16 = f32[2,128,128]{1,2,0:T(8,128)S(1)} custom-call(f32[2,128,128]{2,1,0:T(8,128)S(1)} %get-tuple-element.27), custom_call_target="InvertDiagBlocksLowerTriangular" | custom-call | tf_op jit(solution)/shard_map/jit(_solve_triangular)/triangular_solve | solution.py:91
  733.7 0.4 fusion.8
  734.1 2.5 tile.5
  736.6 10.0 %all-to-all-start.1 = ((f32[64,64,256]{2,1,0:T(8,128)}), f32[64,64,256]{2,1,0:T(8,128)}, u32[]{:S(2)}, u32[]{:S(2)}) async-start(f32[64,64,256]{2,1,0:T(8,128)} %tile.5), calls=%async_computation.1 | async-start | bytes 8388608 | tf_op jit(solution)/shard_map/all_to_all | solution.py:15
  746.6 0.7 sort.32
  747.9 0.4 convolution_subtract_fusion.2
  748.3 0.6 gather_fusion.5
  748.9 0.6 gather_fusion.1
  749.5 0.7 pad_maximum_fusion.3
  750.3 0.7 broadcast_select_fusion.2
  751.0 0.9 bitcast_select_fusion
  751.9 90.6 %all-to-all-done.1 = f32[64,64,256]{2,1,0:T(8,128)} async-done(((f32[64,64,256]{2,1,0:T(8,128)}), f32[64,64,256]{2,1,0:T(8,128)}, u32[]{:S(2)}, u32[]{:S(2)}) %all-to-all-start.1) | async-done | bytes 4194336 | tf_op jit(solution)/shard_map/all_to_all | solution.py:15
  842.5 12.7 %convolution_subtract_fusion = f32[256,4096]{1,0:T(8,128)} fusion(f32[256,4096]{1,0:T(8,128)} %copy-done.1, f32[256,256]{1,0:T(8,128)S(1)} %fusion.8, f32[4096,256]{1,0:T(8,128)} %bitcast.23), kind=kOutput, calls=%fused_computation.10 | convolution fusion | flops 3222274048 | bytes 12845056 | tf_op jit(solution)/shard_map/dot_general | solution.py:29
  855.2 4.9 gather_fusion.3
  860.1 4.8 broadcast_select_fusion
  (72 shorter events, 5.8 us)
Async XLA Ops:
  7.2 15.9 %copy-start = (f32[256,128]{1,0:T(8,128)S(1)}, f32[256,128]{1,0:T(8,128)}, u32[]{:S(2)}) copy-start(f32[256,128]{1,0:T(8,128)} %param.14) | copy-start | bytes 393220
  7.2 63.8 %all-reduce.8.cloned.1.call-start = ((), (), s32[]{:S(2)}) async-start(), calls=%async_computation.2 | async-start | bytes 524288 | tf_op jit(solution)/shard_map/psum | solution.py:25
  19.6 2.0 copy-start.2
  22.4 234.8 %all-reduce.14.cloned.1.call-start = ((), (), s32[]{:S(2)}) async-start(), calls=%async_computation.5 | async-start | bytes 786432 | tf_op jit(solution)/shard_map/psum | solution.py:89
  71.0 249.1 %copy-start.3 = (f32[256,256]{1,0:T(8,128)S(1)}, f32[256,256]{1,0:T(8,128)}, u32[]{:S(2)}) copy-start(f32[256,256]{1,0:T(8,128)} %all-reduce.8.cloned.1.call-done) | copy-start | bytes 786436
  323.1 11.4 %copy-start.5 = (f32[256,128]{1,0:T(8,128)S(1)}, f32[256,128]{1,0:T(8,128)}, u32[]{:S(2)}) copy-start(f32[256,128]{1,0:T(8,128)} %get-tuple-element.47) | copy-start | bytes 393220
  323.1 105.9 %all-to-all-start = ((f32[64,64,256]{2,1,0:T(8,128)}), f32[64,64,256]{2,1,0:T(8,128)}, u32[]{:S(2)}, u32[]{:S(2)}) async-start(f32[64,64,256]{2,1,0:T(8,128)} %tile.4), calls=%async_computation | async-start | bytes 8388608 | tf_op jit(solution)/shard_map/all_to_all | solution.py:15
  333.0 151.3 %all-reduce.10.cloned.1.call-start = ((), (), s32[]{:S(2)}) async-start(), calls=%async_computation.3 | async-start | bytes 524288 | tf_op jit(solution)/shard_map/psum | solution.py:25
  440.4 2.0 copy-start.1
  443.1 227.2 %all-reduce.12.cloned.1.call-start = ((), (), s32[]{:S(2)}) async-start(), calls=%async_computation.4 | async-start | bytes 786432 | tf_op jit(solution)/shard_map/psum | solution.py:89
  484.4 249.3 %copy-start.4 = (f32[256,256]{1,0:T(8,128)S(1)}, f32[256,256]{1,0:T(8,128)}, u32[]{:S(2)}) copy-start(f32[256,256]{1,0:T(8,128)} %all-reduce.10.cloned.1.call-done) | copy-start | bytes 786436
  736.6 10.9 %copy-start.6 = (f32[256,128]{1,0:T(8,128)S(1)}, f32[256,128]{1,0:T(8,128)}, u32[]{:S(2)}) copy-start(f32[256,128]{1,0:T(8,128)} %get-tuple-element.45) | copy-start | bytes 393220
  736.6 105.9 %all-to-all-start.1 = ((f32[64,64,256]{2,1,0:T(8,128)}), f32[64,64,256]{2,1,0:T(8,128)}, u32[]{:S(2)}, u32[]{:S(2)}) async-start(f32[64,64,256]{2,1,0:T(8,128)} %tile.5), calls=%async_computation.1 | async-start | bytes 8388608 | tf_op jit(solution)/shard_map/all_to_all | solution.py:15
Sparse Core Ops, SparseCore 0:
  22.5 48.4 all-reduce.7
  75.5 181.5 all-reduce.13
  443.3 41.0 all-reduce.9
  488.7 181.5 all-reduce.11
